TPU v7x, 512 devices: a whole 4x4x16 slice. The times are simulated.
512 devices in a mesh: seq: 32 (over x, z_lo), head: 8 (over y, core), enc: 2 (over z_hi).
Axes of the slice: x: 4, y: 4, z: 16 (z_hi: 2, z_lo: 8; z = z_hi * 8 + z_lo), core: 2. Of those that a mesh axis runs over, the one named last changes fastest.
Arguments:
- queries: bfloat16 [10240, 4096], P('seq', ('head', 'enc')), may hold values from -2000 to 2000
- keys: bfloat16 [10240, 4096], P('seq', ('head', 'enc')), may hold values from -2000 to 2000
- values: bfloat16 [10240, 4096], P('seq', ('head', 'enc')), may hold values from -6 to 6
- out_weight: bfloat16 [4096, 5120], P(('head', 'enc'), 'seq'), may hold values from -0.1875 to 0.1875
- q_gain: float32 [4096], P(('head', 'enc')), may hold values from 0.75 to 3
- k_gain: float32 [4096], P(('head', 'enc')), may hold values from 0.75 to 3
- gate: float32 [5120], P(('head', 'enc')), may hold values from 1 to 8
- valid_count: int32 [1], replicated, may hold values from 5120 to 10240
Outputs:
- update: bfloat16 [10240, 5120], P('seq', ('head', 'enc'))
Inputs may be any that keep to these rules, and one draw needn't show every extreme that they name: Key positions from valid_count[0] on are padding and take no weight.
All inputs are finite; a program needn't handle non-finite values.
Results may differ from a plain program's by a relative error of at most 0.015.
The roundings to bfloat16 on the way count: a program that leaves them out, or rounds other values in their place, can miss the bound.
Values may be sent and summed in bfloat16 or wider, within the bound.
No kernel may reach another device: no remote copies, remote signals or barrier semaphores. Data moves between devices by JAX's collectives and lax.ppermute only.
A program may use at most 64 MiB of HBM per device.

v0:
```python
import jax
import jax.numpy as jnp
from jax import lax
from jax.sharding import PartitionSpec as P

HEAD_DIM = 128
epsilon = 1e-06
lowest_score = -1e30


def normalize(matrix, squares, gain_row, feature_count):
    inverse_rms = lax.rsqrt(squares / feature_count + epsilon)
    return (matrix.astype(jnp.float32) * inverse_rms[:, None] * gain_row[None, :]).astype(
        jnp.bfloat16
    )


def absorb(carried, query_heads, key_block, value_block, offset, key_limit):
    running_sum, running_max, running_mass = carried
    scale_factor = query_heads.shape[2] ** (-0.5)
    scores = (
        jnp.einsum("qhd,khd->hqk", query_heads, key_block, preferred_element_type=jnp.float32)
        * scale_factor
    )
    position = offset + jnp.arange(key_block.shape[0], dtype=jnp.int32)
    usable = (position < key_limit)[None, None, :]
    masked = jnp.where(usable, scores, lowest_score)
    new_max = jnp.maximum(running_max, jnp.max(masked, axis=2))
    weights = jnp.where(usable, jnp.exp(masked - new_max[:, :, None]), 0.0)
    factor = jnp.exp(running_max - new_max)
    running_mass = running_mass * factor + jnp.sum(weights, axis=2)
    running_sum = running_sum * factor[:, :, None] + jnp.einsum(
        "hqk,khd->hqd",
        weights.astype(jnp.bfloat16),
        value_block,
        preferred_element_type=jnp.float32,
    )
    return (running_sum, new_max, running_mass)


def absorb_blocks(carried, query_heads, key_rows, value_rows, key_limit):
    row_total = key_rows.shape[0]
    block_size = 512
    block_count = row_total // block_size
    key_blocks = key_rows.reshape((block_count, block_size) + key_rows.shape[1:])
    value_blocks = value_rows.reshape((block_count, block_size) + value_rows.shape[1:])

    def absorb_block(running, triple):
        block_number, key_block, value_block = triple
        return (
            absorb(
                running, query_heads, key_block, value_block, block_number * block_size, key_limit
            ),
            None,
        )

    numbers = jnp.arange(block_count, dtype=jnp.int32)
    carried, _ = lax.scan(absorb_block, carried, (numbers, key_blocks, value_blocks))
    return carried


def visit(carried, query_heads, key_rows, value_rows, key_limit):
    return absorb_blocks(carried, query_heads, key_rows, value_rows, key_limit)


def local(queries, keys, values, out_weight, q_gain, k_gain, gate, valid_count):
    row_count = queries.shape[0]
    local_heads = queries.shape[1] // HEAD_DIM
    feature_count = queries.shape[1] * lax.axis_size(("head", "enc"))
    key_limit = valid_count[0]
    query_squares = jnp.sum(jnp.square(queries.astype(jnp.float32)), axis=1)
    key_squares = jnp.sum(jnp.square(keys.astype(jnp.float32)), axis=1)
    query_totals, key_totals = lax.psum((query_squares, key_squares), ("head", "enc"))
    query_heads = normalize(queries, query_totals, q_gain, feature_count).reshape(
        row_count, local_heads, HEAD_DIM
    )
    key_heads = normalize(keys, key_totals, k_gain, feature_count).reshape(
        row_count, local_heads, HEAD_DIM
    )
    value_heads = values.reshape(row_count, local_heads, HEAD_DIM)
    initial = (
        jnp.zeros((local_heads, row_count, HEAD_DIM), jnp.float32),
        jnp.full((local_heads, row_count), lowest_score, jnp.float32),
        jnp.zeros((local_heads, row_count), jnp.float32),
    )
    running_sum, running_max, running_mass = visit(
        initial,
        query_heads,
        lax.all_gather(key_heads, "seq", axis=0, tiled=True),
        lax.all_gather(value_heads, "seq", axis=0, tiled=True),
        key_limit,
    )
    attended = (running_sum / running_mass[:, :, None]).transpose(1, 0, 2)
    attended = attended.reshape(row_count, local_heads * HEAD_DIM).astype(jnp.bfloat16)
    terms = jnp.dot(
        attended,
        lax.all_gather(out_weight, "seq", axis=1, tiled=True),
        preferred_element_type=jnp.float32,
    )
    summed = lax.psum_scatter(
        terms.astype(jnp.bfloat16), ("head", "enc"), scatter_dimension=1, tiled=True
    ).astype(jnp.float32)
    return (gate[None, :] * summed).astype(jnp.bfloat16)


def solution(mesh):
    placed = (
        P("seq", ("head", "enc")),
        P("seq", ("head", "enc")),
        P("seq", ("head", "enc")),
        P(("head", "enc"), "seq"),
        P(("head", "enc")),
        P(("head", "enc")),
        P(("head", "enc")),
        P(),
    )
    return jax.shard_map(
        local, mesh=mesh, in_specs=placed, out_specs=P("seq", ("head", "enc")), check_vma=False
    )
```

profile of v0, /device:TPU:2, one launch (start us, length us, event | category | flops | bytes accessed | tf_op | source)
XLA Modules:
  0.0 957.6 jit_solution(13073559487828346287)
XLA Ops:
  8.7 78.0 %all-reduce = (f32[320]{0:T(512)S(1)}, f32[320]{0:T(512)S(1)}) all-reduce(f32[320]{0:T(512)S(1)} %fusion.11, f32[320]{0:T(512)S(1)} %fusion.14), channel_id=1, replica_groups=mesh['seq'=32,'head'=8,'enc'=2] {'head','enc'}, use_global_device_ids=true, to_apply=%region_1.0 | all-reduce | flops 640 | bytes 5120 | tf_op jit(solution)/shard_map/psum | solution.py:73
  88.5 1.6 reshape.35
  91.1 214.0 %all-gather.4.cloned.1.call-done = bf16[10240,2,128]{2,1,0:T(2,128)(2,1)} async-done(((bf16[320,2,128]{2,1,0:T(2,128)(2,1)}), bf16[10240,2,128]{2,1,0:T(2,128)(2,1)}) %all-gather.4.cloned.1.call-update) | async-done | bytes 5242896 | tf_op jit(solution)/shard_map/all_gather | solution.py:89
  305.2 242.4 %all-gather.6.cloned.1.call-done = bf16[10240,2,128]{2,1,0:T(2,128)(2,1)} async-done(((bf16[320,2,128]{2,1,0:T(2,128)(2,1)}), bf16[10240,2,128]{2,1,0:T(2,128)(2,1)}) %all-gather.6.cloned.1.call-update) | async-done | bytes 5242896 | tf_op jit(solution)/shard_map/all_gather | solution.py:90
  547.6 92.4 %while.15 = (s32[]{:T(128)}, f32[2,320,128]{2,1,0:T(8,128)S(1)}, f32[2,320]{1,0:T(2,128)S(1)}, f32[2,320]{1,0:T(2,128)S(1)}, s32[20]{0:T(128)S(1)}, /*index=5*/s...) while((s32[]{:T(128)}, f32[2,320,128]{2,1,0:T(8,128)S(1)}, ...), condition=%wide.region_7.8_spmd.clone, body=%wide.region_4.7_spmd.clone.sunk | while | flops 170971264 | bytes 6367397 | solution.py:58
  549.4 1.4 constant_dynamic-slice_fusion.3
  554.1 1.4 constant_dynamic-slice_fusion.3
  558.7 1.4 constant_dynamic-slice_fusion.3
  563.3 1.4 constant_dynamic-slice_fusion.3
  567.9 1.4 constant_dynamic-slice_fusion.3
  572.6 1.4 constant_dynamic-slice_fusion.3
  577.2 1.4 constant_dynamic-slice_fusion.3
  581.8 1.4 constant_dynamic-slice_fusion.3
  586.4 1.4 constant_dynamic-slice_fusion.3
  591.1 1.4 constant_dynamic-slice_fusion.3
  609.5 1.4 constant_dynamic-slice_fusion.3
  623.4 1.4 constant_dynamic-slice_fusion.3
  628.0 1.4 constant_dynamic-slice_fusion.3
  632.7 1.4 constant_dynamic-slice_fusion.3
  637.3 1.4 constant_dynamic-slice_fusion.3
  640.0 136.6 %all-gather.8.cloned.1.call-done = bf16[256,5120]{0,1:T(8,128)(2,1)} async-done(((bf16[256,160]{0,1:T(8,128)(2,1)}), bf16[256,5120]{0,1:T(8,128)(2,1)}) %all-gather.8.cloned.1.call-update) | async-done | bytes 2621456 | tf_op jit(solution)/shard_map/all_gather | solution.py:97
  776.6 2.9 convolution_convert_fusion
  779.6 3.6 copy.29
  783.2 166.0 %reduce-scatter.4.cloned.1.call-done = bf16[320,320]{1,0:T(8,128)(2,1)} async-done(((bf16[5120,320]{1,0:T(8,128)(2,1)}), bf16[320,320]{1,0:T(8,128)(2,1)}) %reduce-scatter.4.cloned.1.call-update) | async-done | bytes 204816
  (193 shorter events, 64.2 us)
Async XLA Ops:
  6.5 84.5 %copy-start.1 = (bf16[320,256]{1,0:T(8,128)(2,1)S(1)}, bf16[320,256]{1,0:T(8,128)(2,1)}, u32[]{:S(2)}) copy-start(bf16[320,256]{1,0:T(8,128)(2,1)} %param.10) | copy-start | bytes 491524
  6.5 84.5 %copy-start.3 = (f32[256]{0:T(256)S(1)}, f32[256]{0:T(256)}, u32[]{:S(2)}) copy-start(f32[256]{0:T(256)} %param.14) | copy-start | bytes 3076
  6.5 298.6 %all-gather.4.cloned.1.call-start = ((), (), s32[]{:S(2)}) async-start(), calls=%async_computation.1 | async-start | bytes 5406720 | tf_op jit(solution)/shard_map/all_gather | solution.py:89
  88.5 459.1 %all-gather.6.cloned.1.call-start = ((), (), s32[]{:S(2)}) async-start(), calls=%async_computation.2 | async-start | bytes 5406720 | tf_op jit(solution)/shard_map/all_gather | solution.py:90
  90.2 686.4 %all-gather.8.cloned.1.call-start = ((), (), s32[]{:S(2)}) async-start(), calls=%async_computation.3 | async-start | bytes 2703360 | tf_op jit(solution)/shard_map/all_gather | solution.py:97
  90.9 858.3 %reduce-scatter.4.cloned.1.call-start = ((), (), s32[]{:S(2)}) async-start(), calls=%async_computation.4 | async-start | bytes 4177920
  640.0 136.6 %copy-start = (f32[2,320,128]{2,1,0:T(8,128)}, f32[2,320,128]{2,1,0:T(8,128)S(1)}, u32[]{:S(2)}) copy-start(f32[2,320,128]{2,1,0:T(8,128)S(1)} %get-tuple-element.53) | copy-start | bytes 983044
  783.2 167.2 %copy-start.2 = (f32[320]{0:T(512)S(1)}, f32[320]{0:T(512)}, u32[]{:S(2)}) copy-start(f32[320]{0:T(512)} %param.16) | copy-start | bytes 3844
Sparse Core Ops, SparseCore 0:
  88.6 216.5 all-gather.3
  307.2 240.2 all-gather.5
  549.6 226.9 all-gather.7
  783.4 165.8 reduce-scatter.3
where the time goes:
time: 959 us; the launch traced here: 958 us
  waiting for transfers between devices  760 us (79%)
  blocking collectives  78 us (8%)
  local copies, waits for them, and re-layouts  46.8 us (5%)
  other arithmetic  25.5 us (3%)
  matrix products  20.2 us (2%)
  loops' own time  14.1 us (1%)
  between operations  13.2 us (1%)
    all_gather x1, waiting for transfers between devices, local(): lax.all_gather(value_heads, 'seq', axis=0, tiled=True)  242 us
    all_gather x1, waiting for transfers between devices, local(): lax.all_gather(key_heads, 'seq', axis=0, tiled=True)  214 us
    unnamed x5, waiting for transfers between devices  167 us
    all_gather x1, waiting for transfers between devices, local(): lax.all_gather(out_weight, 'seq', axis=1, tiled=True)  137 us
    psum x1, blocking collectives, local(): lax.psum((query_squares, key_squares), ('head', 'enc'))  78 us
    dynamic_slice x40, local copies, waits for them, and re-layouts, absorb_blocks(): lax.scan(absorb_block, carried, (numbers, key_blocks, value_blocks))  39.7 us
  transfers between devices with their start and end apart: 4, of which 4 were waited for; matrix products, arithmetic and copies ran while one was open for 8% of the time, Pallas kernels for 0%

commit v1 on v0

--- a/solution.py
+++ b/solution.py
@@ -6,6 +6,11 @@
 HEAD_DIM = 128
 epsilon = 1e-06
 lowest_score = -1e30
+
+
+def axis_by_axis(array, first, second):
+    partial = lax.psum(array, first)
+    return lax.psum(partial, second)
 
 
 def normalize(matrix, squares, gain_row, feature_count):
@@ -70,7 +75,7 @@
     key_limit = valid_count[0]
     query_squares = jnp.sum(jnp.square(queries.astype(jnp.float32)), axis=1)
     key_squares = jnp.sum(jnp.square(keys.astype(jnp.float32)), axis=1)
-    query_totals, key_totals = lax.psum((query_squares, key_squares), ("head", "enc"))
+    query_totals, key_totals = axis_by_axis((query_squares, key_squares), "head", "enc")
     query_heads = normalize(queries, query_totals, q_gain, feature_count).reshape(
         row_count, local_heads, HEAD_DIM
     )

time: 959 us -> 918 us (0.957)
  blocking collectives: 78 us -> 31.6 us
    psum x1 -> x2, blocking collectives: 78 us -> 31.6 us  [the longest x1 16.7 us: axis_by_axis(): return lax.psum(partial, second)]
  transfers between devices with their start and end apart: 4 -> 4, of which waited for: 4 -> 4; matrix products, arithmetic and copies ran while one was open for 8% -> 9% of each run, Pallas kernels for 0% -> 0%
where the time goes in v1:
time: 918 us; the launch traced here: 917 us
  waiting for transfers between devices  766 us (83%)
  local copies, waits for them, and re-layouts  46.8 us (5%)
  blocking collectives  31.6 us (3%)
  other arithmetic  24.5 us (3%)
  matrix products  20.2 us (2%)
  loops' own time  14.1 us (2%)
  between operations  13.2 us (1%)
    all_gather x1, waiting for transfers between devices, local(): lax.all_gather(value_heads, 'seq', axis=0, tiled=True)  242 us
    all_gather x1, waiting for transfers between devices, local(): lax.all_gather(key_heads, 'seq', axis=0, tiled=True)  221 us
    unnamed x5, waiting for transfers between devices  166 us
    all_gather x1, waiting for transfers between devices, local(): lax.all_gather(out_weight, 'seq', axis=1, tiled=True)  137 us
    dynamic_slice x40, local copies, waits for them, and re-layouts, absorb_blocks(): lax.scan(absorb_block, carried, (numbers, key_blocks, value_blocks))  39.7 us
  transfers between devices with their start and end apart: 4, of which 4 were waited for; matrix products, arithmetic and copies ran while one was open for 9% of the time, Pallas kernels for 0%

profile of v1, /device:TPU:2, one launch (start us, length us, event | category | flops | bytes accessed | tf_op | source)
XLA Modules:
  0.0 916.9 jit_solution(6728783029805374470)
XLA Ops:
  7.8 14.9 %all-reduce = (f32[320]{0:T(512)S(1)}, f32[320]{0:T(512)S(1)}) all-reduce(f32[320]{0:T(512)S(1)} %get-tuple-element.140, f32[320]{0:T(512)S(1)} %get-tuple-element.141), channel_id=1, replica_groups=mesh['seq'=32,'head'=8,'enc'=2] {'head'}, use_global_device_ids=true, to_apply=%region_1.0 | all-reduce | flops 640 | bytes 5120 | tf_op jit(solution)/shard_map/psum | solution.py:12
  22.6 16.7 %all-reduce.1 = (f32[320]{0:T(512)S(1)}, f32[320]{0:T(512)S(1)}) all-reduce(f32[320]{0:T(512)S(1)} %get-tuple-element.130, f32[320]{0:T(512)S(1)} %get-tuple-element.131), channel_id=1, replica_groups=mesh['seq'=32,'head'=8,'enc'=2] {'enc'}, use_global_device_ids=true, to_apply=%region_2.0 | all-reduce | flops 640 | bytes 5120 | tf_op jit(solution)/shard_map/psum | solution.py:13
  41.2 1.6 reshape.35
  43.8 221.2 %all-gather.4.cloned.1.call-done = bf16[10240,2,128]{2,1,0:T(2,128)(2,1)} async-done(((bf16[320,2,128]{2,1,0:T(2,128)(2,1)}), bf16[10240,2,128]{2,1,0:T(2,128)(2,1)}) %all-gather.4.cloned.1.call-update) | async-done | bytes 5242896 | tf_op jit(solution)/shard_map/all_gather | solution.py:94
  264.9 242.4 %all-gather.6.cloned.1.call-done = bf16[10240,2,128]{2,1,0:T(2,128)(2,1)} async-done(((bf16[320,2,128]{2,1,0:T(2,128)(2,1)}), bf16[10240,2,128]{2,1,0:T(2,128)(2,1)}) %all-gather.6.cloned.1.call-update) | async-done | bytes 5242896 | tf_op jit(solution)/shard_map/all_gather | solution.py:95
  507.3 92.4 %while.15 = (s32[]{:T(128)}, f32[2,320,128]{2,1,0:T(8,128)S(1)}, f32[2,320]{1,0:T(2,128)S(1)}, f32[2,320]{1,0:T(2,128)S(1)}, s32[20]{0:T(128)S(1)}, /*index=5*/s...) while((s32[]{:T(128)}, f32[2,320,128]{2,1,0:T(8,128)S(1)}, ...), condition=%wide.region_9.10_spmd.clone, body=%wide.region_6.9_spmd.clone.sunk | while | flops 170971264 | bytes 6367397 | solution.py:63
  509.2 1.4 constant_dynamic-slice_fusion.3
  513.8 1.4 constant_dynamic-slice_fusion.3
  518.4 1.4 constant_dynamic-slice_fusion.3
  523.1 1.4 constant_dynamic-slice_fusion.3
  527.7 1.4 constant_dynamic-slice_fusion.3
  532.3 1.4 constant_dynamic-slice_fusion.3
  536.9 1.4 constant_dynamic-slice_fusion.3
  560.1 1.4 constant_dynamic-slice_fusion.3
  564.7 1.4 constant_dynamic-slice_fusion.3
  569.3 1.4 constant_dynamic-slice_fusion.3
  573.9 1.4 constant_dynamic-slice_fusion.3
  583.2 1.4 constant_dynamic-slice_fusion.3
  587.8 1.4 constant_dynamic-slice_fusion.3
  597.0 1.4 constant_dynamic-slice_fusion.3
  599.8 137.2 %all-gather.8.cloned.1.call-done = bf16[256,5120]{0,1:T(8,128)(2,1)} async-done(((bf16[256,160]{0,1:T(8,128)(2,1)}), bf16[256,5120]{0,1:T(8,128)(2,1)}) %all-gather.8.cloned.1.call-update) | async-done | bytes 2621456 | tf_op jit(solution)/shard_map/all_gather | solution.py:102
  737.0 2.9 convolution_convert_fusion
  739.9 3.6 copy.29
  743.6 165.0 %reduce-scatter.4.cloned.1.call-done = bf16[320,320]{1,0:T(8,128)(2,1)} async-done(((bf16[5120,320]{1,0:T(8,128)(2,1)}), bf16[320,320]{1,0:T(8,128)(2,1)}) %reduce-scatter.4.cloned.1.call-update) | async-done | bytes 204816
  (194 shorter events, 64.6 us)
Async XLA Ops:
  6.5 37.1 %copy-start.1 = (bf16[320,256]{1,0:T(8,128)(2,1)S(1)}, bf16[320,256]{1,0:T(8,128)(2,1)}, u32[]{:S(2)}) copy-start(bf16[320,256]{1,0:T(8,128)(2,1)} %param.10) | copy-start | bytes 491524
  6.5 37.1 %copy-start.3 = (f32[256]{0:T(256)S(1)}, f32[256]{0:T(256)}, u32[]{:S(2)}) copy-start(f32[256]{0:T(256)} %param.14) | copy-start | bytes 3076
  6.5 258.4 %all-gather.4.cloned.1.call-start = ((), (), s32[]{:S(2)}) async-start(), calls=%async_computation.1 | async-start | bytes 5406720 | tf_op jit(solution)/shard_map/all_gather | solution.py:94
  41.1 466.2 %all-gather.6.cloned.1.call-start = ((), (), s32[]{:S(2)}) async-start(), calls=%async_computation.2 | async-start | bytes 5406720 | tf_op jit(solution)/shard_map/all_gather | solution.py:95
  42.8 694.2 %all-gather.8.cloned.1.call-start = ((), (), s32[]{:S(2)}) async-start(), calls=%async_computation.3 | async-start | bytes 2703360 | tf_op jit(solution)/shard_map/all_gather | solution.py:102
  43.5 865.0 %reduce-scatter.4.cloned.1.call-start = ((), (), s32[]{:S(2)}) async-start(), calls=%async_computation.4 | async-start | bytes 4177920
  599.8 137.2 %copy-start = (f32[2,320,128]{2,1,0:T(8,128)}, f32[2,320,128]{2,1,0:T(8,128)S(1)}, u32[]{:S(2)}) copy-start(f32[2,320,128]{2,1,0:T(8,128)S(1)} %get-tuple-element.53) | copy-start | bytes 983044
  743.5 166.1 %copy-start.2 = (f32[320]{0:T(512)S(1)}, f32[320]{0:T(512)}, u32[]{:S(2)}) copy-start(f32[320]{0:T(512)} %param.16) | copy-start | bytes 3844
Sparse Core Ops, SparseCore 0:
  41.2 223.6 all-gather.3
  267.0 240.2 all-gather.5
  509.4 227.5 all-gather.7
  743.7 164.7 reduce-scatter.3
